TPU v7x, 256 devices: a whole 4x4x8 slice. The times are simulated.
256 devices in a mesh: query: 32 (over y, x, core), feat: 8 (over z).
Axes of the slice: x: 4, y: 4, z: 8, core: 2. Of those that a mesh axis runs over, the one named last changes fastest.
Arguments:
- scores: float32 [262144], P(('query', 'feat')), may hold values from -6 to 6
- labels: int32 [262144], P('query'), may hold values from 0 to 4
- leaves: int32 [262144], P(('query', 'feat')), may hold values from 0 to 1023
- bins: int32 [262144, 256], P(('query', 'feat')), may hold values from 0 to 255
- lengths: int32 [32, 32], P('query'), may hold values from 1 to 1024, 8192 in all within a row
- owner: int32 [256], replicated, may hold values from 0 to 255, each once
Outputs:
- lambdas: float32 [2, 262144], P(None, ('query', 'feat'))
- leaf_values: float32 [1024], replicated
- score_step: float32 [262144], P(('query', 'feat'))
- histograms: float32 [3, 65536], P(None, ('query', 'feat'))
Inputs may be any that keep to these rules, and one draw needn't show every extreme that they name: `lengths`: each row sums to 8192. `owner`: a permutation; the p-th device of query+feat, in that order, holds the histograms of the features owner[j] for p <= j < (p + 1).
All inputs are finite; a program needn't handle non-finite values.
Results may differ from a plain program's by a relative error of at most 0.0003.
Values sent between devices are 32-bit elements; how exact they have to be, the bound alone decides.
A program may use at most 128 MiB of HBM per device.

v0:
```python
import jax
import jax.numpy as jnp
from jax import lax
from jax.sharding import PartitionSpec as P

BINS = 256
LEAVES = 1024
TILE_ROWS = 512
WINDOW = 1536
lasso_penalty = 1.0
ridge_penalty = 1.0
shrinkage = 0.1
group_width = 8


def query_of(lengths_row, count):
    bounds = jnp.cumsum(lengths_row)
    places = jnp.arange(count, dtype=jnp.int32)
    return jnp.searchsorted(bounds, places, side="right")


def place_in_query(sorted_ids):
    places = jnp.arange(sorted_ids.shape[0], dtype=jnp.int32)
    first = jnp.concatenate([jnp.ones((1,), dtype=jnp.bool_), sorted_ids[1:] != sorted_ids[:-1]])
    starts = lax.cummax(jnp.where(first, places, 0), axis=0)
    return places - starts


def query_stats(values, grades, query_ids, count):
    order = jnp.lexsort((-values, query_ids))
    ranked = place_in_query(query_ids[order])
    standing = jnp.zeros(values.shape, jnp.int32).at[order].set(ranked)
    discount = 1.0 / jnp.log2(2.0 + standing.astype(jnp.float32))
    ideal_order = jnp.lexsort((-grades, query_ids))
    ideal_ids = query_ids[ideal_order]
    ideal_place = place_in_query(ideal_ids)
    worth = jnp.exp2(grades[ideal_order].astype(jnp.float32)) - 1.0
    terms = worth / jnp.log2(2.0 + ideal_place.astype(jnp.float32))
    slots = jnp.where(ideal_ids >= 0, ideal_ids, count)
    ideal = jax.ops.segment_sum(terms, slots, num_segments=count + 1)
    usable = ideal > 0.5
    inverse = jnp.where(usable, 1.0 / jnp.where(usable, ideal, 1.0), 0.0)
    return (discount, inverse[jnp.where(query_ids >= 0, query_ids, count)])


def pair_block(row_part, col_part):
    row_score, row_grade, row_query, row_discount, row_inverse, row_place = row_part
    col_score, col_grade, col_query, col_discount, col_place = col_part
    keep = (row_query[:, None] == col_query[None, :]) & (row_query[:, None] >= 0)
    keep = keep & (col_place[None, :] > row_place[:, None])
    row_worth = jnp.exp2(row_grade.astype(jnp.float32))
    col_worth = jnp.exp2(col_grade.astype(jnp.float32))
    signs = jnp.sign(row_grade[:, None] - col_grade[None, :]).astype(jnp.float32)
    change = (
        jnp.abs(row_worth[:, None] - col_worth[None, :])
        * jnp.abs(row_discount[:, None] - col_discount[None, :])
        * row_inverse[:, None]
    )
    chance = jax.nn.sigmoid(-signs * (row_score[:, None] - col_score[None, :]))
    push = jnp.where(keep, change * chance, 0.0) * signs
    bend = jnp.where(keep, change * chance * (1.0 - chance), 0.0)
    return (
        -jnp.sum(push, axis=1),
        jnp.sum(bend, axis=1),
        jnp.sum(push, axis=0),
        jnp.sum(bend, axis=0),
    )


def add_into(total, piece, start):
    current = lax.dynamic_slice_in_dim(total, start, piece.shape[0])
    return lax.dynamic_update_slice_in_dim(total, current + piece, start, 0)


def leaf_newton(sums):
    total_grad = sums[0]
    total_curv = sums[1]
    return (
        -jnp.sign(total_grad)
        * jnp.maximum(jnp.abs(total_grad) - lasso_penalty, 0.0)
        / (total_curv + ridge_penalty)
    )


def histogram_of(gradient, curvature, bins, owner):
    weights = jnp.stack([gradient, curvature, jnp.ones_like(gradient)])
    ordered = jnp.take(bins, owner, axis=1)
    groups = ordered.shape[1] // group_width
    grouped = ordered.reshape(ordered.shape[0], groups, group_width).transpose(1, 0, 2)
    levels = jnp.arange(BINS, dtype=jnp.int32)

    def one_group(group_bins):
        onehot = (group_bins[:, :, None] == levels[None, None, :]).astype(jnp.bfloat16)
        return jnp.einsum(
            "cd,dgb->cgb", weights, onehot.astype(jnp.float32), precision=lax.Precision.HIGHEST
        )

    parts = lax.map(one_group, grouped)
    return parts.transpose(1, 0, 2, 3).reshape(3, -1)


def local(scores, labels, leaves, bins, lengths, owner):
    feat_count = lax.axis_size("feat")
    feat_pos = lax.axis_index("feat")
    own_rows = scores.shape[0]
    block_rows = labels.shape[0]
    lengths_row = lengths[0]
    queries = lengths_row.shape[0]
    block_ids = query_of(lengths_row, block_rows)
    whole = lax.all_gather(scores, "feat", axis=0, tiled=True)
    discount, inverse = query_stats(whole, labels, block_ids, queries)
    padded = (
        jnp.pad(whole, (0, WINDOW)),
        jnp.pad(labels, (0, WINDOW)),
        jnp.pad(block_ids, (0, WINDOW), constant_values=-1),
        jnp.pad(discount, (0, WINDOW)),
        jnp.pad(inverse, (0, WINDOW)),
        jnp.arange(block_rows + WINDOW, dtype=jnp.int32),
    )

    def visit(tile_index, carry):
        acc_grad, acc_curv = carry
        start = (tile_index * feat_count + feat_pos) * TILE_ROWS
        row_part = tuple((lax.dynamic_slice_in_dim(item, start, TILE_ROWS) for item in padded))
        col_part = tuple(
            (lax.dynamic_slice_in_dim(padded[which], start, WINDOW) for which in (0, 1, 2, 3, 5))
        )
        row_grad, row_curv, col_grad, col_curv = pair_block(row_part, col_part)
        acc_grad = add_into(add_into(acc_grad, col_grad, start), row_grad, start)
        acc_curv = add_into(add_into(acc_curv, col_curv, start), row_curv, start)
        return (acc_grad, acc_curv)

    empty = jnp.zeros((block_rows + WINDOW,), jnp.float32)
    acc_grad, acc_curv = lax.fori_loop(0, own_rows // TILE_ROWS, visit, (empty, empty))
    partial_sums = jnp.stack([acc_grad[:block_rows], acc_curv[:block_rows]])
    lambdas = lax.psum_scatter(partial_sums, "feat", scatter_dimension=1, tiled=True)
    table = (leaves[:, None] == jnp.arange(LEAVES, dtype=jnp.int32)[None, :]).astype(jnp.float32)
    leaf_part = jnp.dot(lambdas, table, precision=lax.Precision.HIGHEST)
    leaf_values = leaf_newton(lax.psum(leaf_part, ("query", "feat")))
    score_step = shrinkage * leaf_values[leaves]
    partial_hist = histogram_of(lambdas[0], lambdas[1], bins, owner)
    histograms = lax.psum_scatter(partial_hist, ("query", "feat"), scatter_dimension=1, tiled=True)
    return (lambdas, leaf_values, score_step, histograms)


def solution(mesh):
    in_specs = (
        P(("query", "feat")),
        P("query"),
        P(("query", "feat")),
        P(("query", "feat"), None),
        P("query", None),
        P(),
    )
    out_specs = (P(None, ("query", "feat")), P(), P(("query", "feat")), P(None, ("query", "feat")))
    return jax.shard_map(local, mesh=mesh, in_specs=in_specs, out_specs=out_specs, check_vma=False)
```

profile of v0, /device:TPU:0, one launch (start us, length us, event | category | flops | bytes accessed | tf_op | source)
XLA Modules:
  0.0 2085.9 jit_solution(8405152336099937605)
XLA Ops:
  8.9 250.6 %while.53 = (s32[]{:T(128)}, u32[8192]{0:T(1024)S(1)}, u32[8192]{0:T(1024)S(1)}, s32[32]{0:T(128)S(1)}, s32[]{:T(128)}, /*index=5*/s32[]{:T(128)}) while((s32[]{:T(128)}, u32[8192]{0:T(1024)S(1)}, u32[8192]{0:T(1024)S(1)}, s32[32]{0:T(128)S(1)}, s32[]{:T(128)}, /*index=5*/s32[]{:T(128)}) %tuple.163), condition=%wide.region_2.3_spmd.clone, body=%wide.region_1.2_spmd.clone.sunk | while | flops 1130499 | bytes 262736 | solution.py:19
  10.4 20.1 fusion.52
  30.5 20.1 fusion.51
  52.1 20.1 fusion.52
  72.3 20.1 fusion.51
  93.9 20.1 fusion.52
  114.0 20.1 fusion.51
  135.6 20.1 fusion.52
  155.8 20.1 fusion.51
  177.4 20.1 fusion.52
  197.6 20.1 fusion.51
  219.2 20.1 fusion.52
  239.3 20.1 fusion.51
  259.5 7.2 sort.47
  266.7 45.5 %gather_fusion.1 = s32[8192]{0:T(1024)S(1)} fusion(s32[8192]{0:T(1024)S(1)} %convert_element_type.47, s32[8192]{0:T(1024)S(1)} %fusion.18), kind=kCustom, calls=%fused_computation.1 | custom fusion | bytes 98304 | tf_op jit(solution)/shard_map/gather | solution.py:35
  312.3 45.5 %gather_fusion.2 = s32[8192]{0:T(1024)S(1)} fusion(s32[8192]{0:T(1024)S(1)} %copy-done, s32[8192]{0:T(1024)S(1)} %fusion.18), kind=kCustom, calls=%fused_computation.2 | custom fusion | bytes 98304 | tf_op jit(solution)/shard_map/gather | solution.py:37
  357.9 26.5 %all_gather.3 = f32[8192]{0:T(1024)S(1)} all-gather(f32[1024]{0:T(1024)S(1)} %copy-done.5), channel_id=1, replica_groups=mesh['query'=32,'feat'=8] {'feat'}, dimensions={0}, use_global_device_ids=true | all-gather | bytes 36864 | tf_op jit(solution)/shard_map/all_gather | solution.py:110
  384.4 7.5 sort.46
  391.9 45.5 %gather_fusion = s32[8192]{0:T(1024)S(1)} fusion(s32[8192]{0:T(1024)S(1)} %convert_element_type.47, s32[8192]{0:T(1024)S(1)} %get-tuple-element.414), kind=kCustom, calls=%fused_computation | custom fusion | bytes 98304 | tf_op jit(solution)/shard_map/gather | solution.py:31
  438.5 57.0 %scatter_custom_fusion.1 = f32[33]{0:T(128)S(1)} fusion(s32[8192]{0:T(1024)S(1)} %bitcast.202, f32[8192]{0:T(1024)S(1)} %fusion.23, f32[]{:T(128)} %constant.151.clone.1), kind=kCustom, calls=%fused_computation.86 | custom fusion | flops 8192 | bytes 136 | tf_op jit(solution)/shard_map/scatter-add | solution.py:40
  497.6 30.5 %scatter_custom_fusion = s32[8192]{0:T(1024)S(1)} fusion(s32[8192]{0:T(1024)S(1)} %get-tuple-element.415, s32[8192]{0:T(1024)S(1)} %bitcast_subtract_fusion.1, s32[]{:T(128)} %copy.60), kind=kCustom, calls=%fused_computation.74 | custom fusion | bytes 32772 | tf_op jit(solution)/shard_map/scatter | solution.py:32
  528.2 20.7 select_select_fusion.4
  549.0 12.7 while.51
  549.8 4.9 fusion.46
  556.2 4.9 fusion.46
  561.8 2.6 copy.22
  567.2 52.0 %reduce-scatter.7.cloned.1.call-done = f32[1024,2]{1,0:T(8,128)} async-done(((f32[8192,2]{1,0:T(8,128)}), f32[1024,2]{1,0:T(8,128)}) %reduce-scatter.7.cloned.1.call-update) | async-done | bytes 8208
  621.0 102.5 %while.52 = (s32[]{:T(128)}, f32[32,3,8,256]{3,1,2,0:T(4,128)S(1)}, s32[32,1024,8]{1,2,0:T(8,128)S(1)}, f32[3,1024]{1,0:T(4,128)S(1)}, s32[]{:T(128)}) while((s32[]{:T(128)}, f32[32,3,8,256]{3,1,2,0:T(4,128)S(1)}, s32[32,1024,8]{1,2,0:T(8,128)S(1)}, f32[3,1024]{1,0:T(4,128)S(1)}, s32[]{:T(128)}) %tuple.169), condition=%wide.region_20.21_spmd.clone, body=%wide.region_19.20_spmd.clone.sunk | while | flops 77594624 | bytes 147533 | solution.py:98
  621.1 3.2 fusion.48
  624.2 3.2 fusion.48
  627.4 3.2 fusion.48
  630.6 3.2 fusion.48
  633.8 3.2 fusion.48
  637.1 3.2 fusion.48
  640.3 3.2 fusion.48
  643.5 3.2 fusion.48
  646.7 3.2 fusion.48
  649.9 3.2 fusion.48
  653.1 3.2 fusion.48
  656.3 3.2 fusion.48
  659.5 3.2 fusion.48
  662.7 3.2 fusion.48
  665.9 3.2 fusion.48
  669.1 3.2 fusion.48
  672.3 3.2 fusion.48
  675.5 3.2 fusion.48
  678.7 3.2 fusion.48
  681.9 3.2 fusion.48
  685.1 3.2 fusion.48
  688.3 3.2 fusion.48
  691.5 3.2 fusion.48
  694.7 3.2 fusion.48
  697.9 3.2 fusion.48
  701.1 3.2 fusion.48
  704.3 3.2 fusion.48
  707.5 3.2 fusion.48
  710.7 3.2 fusion.48
  713.9 3.2 fusion.48
  717.1 3.2 fusion.48
  720.3 3.2 fusion.48
  723.5 16.0 copy.24
  742.1 78.0 %psum.7 = f32[2,1024]{1,0:T(2,128)S(1)} all-reduce(f32[2,1024]{1,0:T(2,128)S(1)} %fusion.15), channel_id=1, replica_groups=mesh['query'=32,'feat'=8] {'query','feat'}, use_global_device_ids=true, to_apply=%region_18.19 | all-reduce | flops 2048 | bytes 16384 | tf_op jit(solution)/shard_map/psum | solution.py:139
  820.1 4.5 gather_fusion.3
  825.2 1252.3 %reduce-scatter.9.cloned.1.call-done = f32[256,3]{1,0:T(8,128)} async-done(((f32[65536,3]{1,0:T(8,128)}), f32[256,3]{1,0:T(8,128)}) %reduce-scatter.9.cloned.1.call-update) | async-done | bytes 3088
  (154 shorter events, 26.0 us)
Async XLA Ops:
  7.2 612.1 %reduce-scatter.7.cloned.1.call-start = ((), (), s32[]{:S(2)}) async-start(), calls=%async_computation.2 | async-start | bytes 4718592
  266.7 45.6 %copy-start = (s32[8192]{0:T(1024)S(1)}, s32[8192]{0:T(1024)}, u32[]{:S(2)}) copy-start(s32[8192]{0:T(1024)} %param.13) | copy-start | bytes 98308
  312.3 45.6 %copy-start.5 = (f32[1024]{0:T(1024)S(1)}, f32[1024]{0:T(1024)}, u32[]{:S(2)}) copy-start(f32[1024]{0:T(1024)} %param.12) | copy-start | bytes 12292
  564.4 0.7 copy-start.7
  564.4 1.2 copy-start.2
  564.4 1513.0 %reduce-scatter.9.cloned.1.call-start = ((), (), s32[]{:S(2)}) async-start(), calls=%async_computation.3 | async-start | bytes 33685504
  620.4 0.6 copy-start.4
  739.6 0.7 copy-start.6
  739.6 1.1 copy-start.3
  820.1 1259.0 %copy-start.1 = (f32[1,1024]{1,0:T(1,128)}, f32[1,1024]{1,0:T(1,128)S(1)}, u32[]{:S(2)}) copy-start(f32[1,1024]{1,0:T(1,128)S(1)} %fusion.31) | copy-start | bytes 12292
Sparse Core Ops, SparseCore 0:
  564.5 54.6 reduce-scatter.6
  739.7 1337.7 reduce-scatter.8
where the time goes:
time: 2090 us
  waiting for transfers between devices  1300 us (62%)
  other arithmetic  349 us (17%)
  local copies, waits for them, and re-layouts  210 us (10%)
  blocking collectives  105 us (5%)
  matrix products  104 us (5%)
    unnamed x4, waiting for transfers between devices  1300 us
    select_n x12, other arithmetic, query_of(): return jnp.searchsorted(bounds, places, side='right')  242 us
    dot_general x32, matrix products, one_group(): jnp.einsum('cd,dgb->cgb', weights, onehot.astype(jnp.float32), precision=...  102 us
    psum x1, blocking collectives, local(): leaf_values = leaf_newton(lax.psum(leaf_part, ('query', 'feat')))  78 us
    scatter-add x1, other arithmetic, query_stats(): ideal = jax.ops.segment_sum(terms, slots, num_segments=count + 1)  57 us
    gather x1, local copies, waits for them, and re-layouts, query_stats(): ideal_ids = query_ids[ideal_order]  45.5 us
    gather x1, local copies, waits for them, and re-layouts, query_stats(): worth = jnp.exp2(grades[ideal_order].astype(jnp.float32)) - 1.0  45.5 us
    gather x1, local copies, waits for them, and re-layouts, query_stats(): ranked = place_in_query(query_ids[order])  45.5 us
  transfers between devices with their start and end apart: 2, of which 2 were waited for; matrix products, arithmetic and copies ran while one was open for 0% of the time, Pallas kernels for 0%

commit v1 on v0

--- a/solution.py
+++ b/solution.py
@@ -136,7 +136,7 @@
     lambdas = lax.psum_scatter(partial_sums, "feat", scatter_dimension=1, tiled=True)
     table = (leaves[:, None] == jnp.arange(LEAVES, dtype=jnp.int32)[None, :]).astype(jnp.float32)
     leaf_part = jnp.dot(lambdas, table, precision=lax.Precision.HIGHEST)
-    leaf_values = leaf_newton(lax.psum(leaf_part, ("query", "feat")))
+    leaf_values = leaf_newton(jnp.sum(lax.all_gather(leaf_part, ("query", "feat")), axis=0))
     score_step = shrinkage * leaf_values[leaves]
     partial_hist = histogram_of(lambdas[0], lambdas[1], bins, owner)
     histograms = lax.psum_scatter(partial_hist, ("query", "feat"), scatter_dimension=1, tiled=True)

time: 2090 us -> 2200 us (1.053)
  waiting for transfers between devices: 1300 us -> 1490 us
  blocking collectives: 105 us -> 26.5 us
    all_gather x0 -> x1, waiting for transfers between devices: none -> 98.9 us  [local(): lax.all_gather(leaf_part, ('query', 'feat'))]
    unnamed x4 -> x5, waiting for transfers between devices: 1300 us -> 1390 us
    psum x1 -> x0, blocking collectives: 78 us -> none  [local(): leaf_values = leaf_newton(lax.psum(leaf_part, ('query', 'feat')))]
  transfers between devices with their start and end apart: 2 -> 3, of which waited for: 2 -> 3; matrix products, arithmetic and copies ran while one was open for 0% -> 0% of each run, Pallas kernels for 0% -> 0%
where the time goes in v1:
time: 2200 us; the launch traced here: 2190 us
  waiting for transfers between devices  1490 us (68%)
  other arithmetic  351 us (16%)
  local copies, waits for them, and re-layouts  210 us (10%)
  matrix products  104 us (5%)
  blocking collectives  26.5 us (1%)
    unnamed x5, waiting for transfers between devices  1390 us
    select_n x12, other arithmetic, query_of(): return jnp.searchsorted(bounds, places, side='right')  242 us
    dot_general x32, matrix products, one_group(): jnp.einsum('cd,dgb->cgb', weights, onehot.astype(jnp.float32), precision=...  102 us
    all_gather x1, waiting for transfers between devices, local(): lax.all_gather(leaf_part, ('query', 'feat'))  98.9 us
    scatter-add x1, other arithmetic, query_stats(): ideal = jax.ops.segment_sum(terms, slots, num_segments=count + 1)  57 us
    gather x1, local copies, waits for them, and re-layouts, query_stats(): ideal_ids = query_ids[ideal_order]  45.5 us
    gather x1, local copies, waits for them, and re-layouts, query_stats(): worth = jnp.exp2(grades[ideal_order].astype(jnp.float32)) - 1.0  45.5 us
    gather x1, local copies, waits for them, and re-layouts, query_stats(): ranked = place_in_query(query_ids[order])  45.5 us
  transfers between devices with their start and end apart: 3, of which 3 were waited for; matrix products, arithmetic and copies ran while one was open for 0% of the time, Pallas kernels for 0%

profile of v1, /device:TPU:0, one launch (start us, length us, event | category | flops | bytes accessed | tf_op | source)
XLA Modules:
  0.0 2193.8 jit_solution(8078160898273132135)
XLA Ops:
  8.9 250.6 %while.53 = (s32[]{:T(128)}, u32[8192]{0:T(1024)S(1)}, u32[8192]{0:T(1024)S(1)}, s32[32]{0:T(128)S(1)}, s32[]{:T(128)}, /*index=5*/s32[]{:T(128)}) while((s32[]{:T(128)}, u32[8192]{0:T(1024)S(1)}, u32[8192]{0:T(1024)S(1)}, s32[32]{0:T(128)S(1)}, s32[]{:T(128)}, /*index=5*/s32[]{:T(128)}) %tuple.163), condition=%wide.region_2.3_spmd.clone, body=%wide.region_1.2_spmd.clone.sunk | while | flops 1130499 | bytes 262736 | solution.py:19
  10.4 20.1 fusion.53
  30.5 20.1 fusion.52
  52.1 20.1 fusion.53
  72.3 20.1 fusion.52
  93.9 20.1 fusion.53
  114.0 20.1 fusion.52
  135.6 20.1 fusion.53
  155.8 20.1 fusion.52
  177.4 20.1 fusion.53
  197.6 20.1 fusion.52
  219.2 20.1 fusion.53
  239.3 20.1 fusion.52
  259.5 7.2 sort.47
  266.7 45.5 %gather_fusion.1 = s32[8192]{0:T(1024)S(1)} fusion(s32[8192]{0:T(1024)S(1)} %convert_element_type.47, s32[8192]{0:T(1024)S(1)} %fusion.19), kind=kCustom, calls=%fused_computation.1 | custom fusion | bytes 98304 | tf_op jit(solution)/shard_map/gather | solution.py:35
  312.3 45.5 %gather_fusion.2 = s32[8192]{0:T(1024)S(1)} fusion(s32[8192]{0:T(1024)S(1)} %copy-done, s32[8192]{0:T(1024)S(1)} %fusion.19), kind=kCustom, calls=%fused_computation.2 | custom fusion | bytes 98304 | tf_op jit(solution)/shard_map/gather | solution.py:37
  357.9 26.5 %all_gather.9 = f32[8192]{0:T(1024)S(1)} all-gather(f32[1024]{0:T(1024)S(1)} %copy-done.5), channel_id=1, replica_groups=mesh['query'=32,'feat'=8] {'feat'}, dimensions={0}, use_global_device_ids=true | all-gather | bytes 36864 | tf_op jit(solution)/shard_map/all_gather | solution.py:110
  384.4 7.5 sort.46
  391.9 45.5 %gather_fusion = s32[8192]{0:T(1024)S(1)} fusion(s32[8192]{0:T(1024)S(1)} %convert_element_type.47, s32[8192]{0:T(1024)S(1)} %get-tuple-element.414), kind=kCustom, calls=%fused_computation | custom fusion | bytes 98304 | tf_op jit(solution)/shard_map/gather | solution.py:31
  438.5 57.0 %scatter_custom_fusion.1 = f32[33]{0:T(128)S(1)} fusion(s32[8192]{0:T(1024)S(1)} %bitcast.204, f32[8192]{0:T(1024)S(1)} %fusion.24, f32[]{:T(128)} %constant.151.clone.1), kind=kCustom, calls=%fused_computation.87 | custom fusion | flops 8192 | bytes 136 | tf_op jit(solution)/shard_map/scatter-add | solution.py:40
  497.6 30.5 %scatter_custom_fusion = s32[8192]{0:T(1024)S(1)} fusion(s32[8192]{0:T(1024)S(1)} %get-tuple-element.415, s32[8192]{0:T(1024)S(1)} %bitcast_subtract_fusion.1, s32[]{:T(128)} %copy.61), kind=kCustom, calls=%fused_computation.75 | custom fusion | bytes 32772 | tf_op jit(solution)/shard_map/scatter | solution.py:32
  528.2 20.7 select_select_fusion.4
  549.0 12.7 while.51
  549.8 4.9 fusion.47
  556.2 4.9 fusion.47
  561.8 2.6 copy.22
  567.2 52.0 %reduce-scatter.7.cloned.1.call-done = f32[1024,2]{1,0:T(8,128)} async-done(((f32[8192,2]{1,0:T(8,128)}), f32[1024,2]{1,0:T(8,128)}) %reduce-scatter.7.cloned.1.call-update) | async-done | bytes 8208
  621.1 102.5 %while.52 = (s32[]{:T(128)}, f32[32,3,8,256]{3,1,2,0:T(4,128)S(1)}, s32[32,1024,8]{1,2,0:T(8,128)S(1)}, f32[3,1024]{1,0:T(4,128)S(1)}, s32[]{:T(128)}) while((s32[]{:T(128)}, f32[32,3,8,256]{3,1,2,0:T(4,128)S(1)}, s32[32,1024,8]{1,2,0:T(8,128)S(1)}, f32[3,1024]{1,0:T(4,128)S(1)}, s32[]{:T(128)}) %tuple.169), condition=%wide.region_20.21_spmd.clone, body=%wide.region_19.20_spmd.clone.sunk | while | flops 77594624 | bytes 147533 | solution.py:98
  621.1 3.2 fusion.49
  624.2 3.2 fusion.49
  627.4 3.2 fusion.49
  630.6 3.2 fusion.49
  633.9 3.2 fusion.49
  637.1 3.2 fusion.49
  640.3 3.2 fusion.49
  643.5 3.2 fusion.49
  646.7 3.2 fusion.49
  649.9 3.2 fusion.49
  653.1 3.2 fusion.49
  656.3 3.2 fusion.49
  659.5 3.2 fusion.49
  662.7 3.2 fusion.49
  665.9 3.2 fusion.49
  669.1 3.2 fusion.49
  672.3 3.2 fusion.49
  675.5 3.2 fusion.49
  678.7 3.2 fusion.49
  681.9 3.2 fusion.49
  685.1 3.2 fusion.49
  688.3 3.2 fusion.49
  691.5 3.2 fusion.49
  694.7 3.2 fusion.49
  697.9 3.2 fusion.49
  701.1 3.2 fusion.49
  704.3 3.2 fusion.49
  707.5 3.2 fusion.49
  710.7 3.2 fusion.49
  713.9 3.2 fusion.49
  717.1 3.2 fusion.49
  720.3 3.2 fusion.49
  723.5 16.0 copy.24
  742.7 1336.7 %reduce-scatter.9.cloned.1.call-done = f32[256,3]{1,0:T(8,128)} async-done(((f32[65536,3]{1,0:T(8,128)}), f32[256,3]{1,0:T(8,128)}) %reduce-scatter.9.cloned.1.call-update) | async-done | bytes 3088
  2081.0 98.9 %all-gather.4.cloned.1.call-done = f32[256,2,1024]{2,1,0:T(2,128)} async-done(((f32[1,2,1024]{2,1,0:T(2,128)}), f32[256,2,1024]{2,1,0:T(2,128)}) %all-gather.4.cloned.1.call-update) | async-done | bytes 2097168 | tf_op jit(solution)/shard_map/all_gather | solution.py:139
  2182.1 4.5 gather_fusion.3
  (157 shorter events, 28.8 us)
Async XLA Ops:
  7.2 612.1 %reduce-scatter.7.cloned.1.call-start = ((), (), s32[]{:S(2)}) async-start(), calls=%async_computation.3 | async-start | bytes 4718592
  266.7 45.6 %copy-start = (s32[8192]{0:T(1024)S(1)}, s32[8192]{0:T(1024)}, u32[]{:S(2)}) copy-start(s32[8192]{0:T(1024)} %param.13) | copy-start | bytes 98308
  312.3 45.6 %copy-start.5 = (f32[1024]{0:T(1024)S(1)}, f32[1024]{0:T(1024)}, u32[]{:S(2)}) copy-start(f32[1024]{0:T(1024)} %param.12) | copy-start | bytes 12292
  564.4 0.7 copy-start.7
  564.4 1.2 copy-start.2
  564.4 1515.0 %reduce-scatter.9.cloned.1.call-start = ((), (), s32[]{:S(2)}) async-start(), calls=%async_computation.4 | async-start | bytes 33685504
  620.4 0.6 copy-start.4
  739.6 1.0 copy-start.3
  739.6 1.0 copy-start.6
  739.6 1440.3 %all-gather.4.cloned.1.call-start = ((), (), s32[]{:S(2)}) async-start(), calls=%async_computation.2 | async-start | bytes 2105344 | tf_op jit(solution)/shard_map/all_gather | solution.py:139
  2182.1 5.1 copy-start.1
Sparse Core Ops, SparseCore 0:
  564.5 54.6 reduce-scatter.6
  739.7 1339.6 reduce-scatter.8
  2083.1 96.6 all-gather.3
